TPU v7x, 32 devices: a whole 2x2x4 slice. The times are simulated.
32 devices in a mesh: dp: 4 (over x, core), fsdp: 8 (over z, y).
Axes of the slice: x: 2, y: 2, z: 4, core: 2. Of those that a mesh axis runs over, the one named last changes fastest.
Arguments:
- block_input: bfloat16 [32, 512, 576], P(('dp', 'fsdp')), may hold values from -18 to 18
- lengths: int32 [32], P(('dp', 'fsdp')), may hold values from 128 to 512, as said below
- attention_gain: float32 [576], replicated, may hold values from 0.1 to 1.9
- query_weight: bfloat16 [576, 576], P('dp', 'fsdp'), may hold values from -0.25 to 0.25
- key_matrix: bfloat16 [576, 192], P('dp', 'fsdp'), may hold values from -0.25 to 0.25
- value_matrix: bfloat16 [576, 192], P('dp', 'fsdp'), may hold values from -0.25 to 0.25
- output_weight: bfloat16 [576, 576], P('dp', 'fsdp'), may hold values from -1 to 1
- mlp_gain: float32 [576], replicated, may hold values from 0.1 to 1.9
- gate_weight: bfloat16 [576, 1536], P('dp', 'fsdp'), may hold values from -0.25 to 0.25
- up_weight: bfloat16 [576, 1536], P('dp', 'fsdp'), may hold values from -0.25 to 0.25
- down_weight: bfloat16 [1536, 576], P('dp', 'fsdp'), may hold values from -0.15625 to 0.15625
- cotangent: bfloat16 [32, 512, 576], P(('dp', 'fsdp')), may hold values from -6 to 6
Outputs:
- block_output: bfloat16 [32, 512, 576], P(('dp', 'fsdp'))
- input_grad: float32 [32, 512, 576], P(('dp', 'fsdp'))
- grad_attention_gain: float32 [576], replicated
- grad_query: float32 [576, 576], P('dp', 'fsdp')
- grad_key: float32 [576, 192], P('dp', 'fsdp')
- grad_value: float32 [576, 192], P('dp', 'fsdp')
- grad_output: float32 [576, 576], P('dp', 'fsdp')
- grad_mlp_gain: float32 [576], replicated
- grad_gate: float32 [576, 1536], P('dp', 'fsdp')
- grad_up: float32 [576, 1536], P('dp', 'fsdp')
- grad_down: float32 [1536, 576], P('dp', 'fsdp')
- stream_rms: float32 [2, 3], replicated
Inputs may be any that keep to these rules, and one draw needn't show every extreme that they name: `lengths`: slots are filled from their first place; some slot has exactly 512 valid tokens and some slot exactly 128.
All inputs are finite; a program needn't handle non-finite values.
Results may differ from a plain program's by a relative error of at most 0.022.
Values may be sent and summed in bfloat16 or wider, within the bound.
A program may use at most 192 MiB of HBM per device.

v0:
```python
import functools
import jax
import jax.numpy as jnp
import numpy as np
from jax import lax
from jax.experimental import pallas as pl
from jax.experimental.pallas import tpu as pltpu
from jax.sharding import PartitionSpec as P

D = 576
NQ = 9
NK = 3
GROUP = NQ // NK
H = 64
HALF = H // 2
FF = 1536
T = 512
NF = 8
QB = D // NF
KB = NK * H // NF
FB = FF // NF
EPS = 1e-05
ROPE_BASE = 10000.0
SCALE = H ** (-0.5)
NEG = -1e30
BLK = 256
VMEM_LIMIT = 63 * 2**20
ROWS = D // 4
LANES = FF // 4
OW = QB - 8
BF = jnp.bfloat16
F32 = jnp.float32


def dot(a, b, ca, cb):
    return lax.dot_general(a, b, (((ca,), (cb,)), ((), ())), preferred_element_type=F32)


def rope_tables():
    inverse = ROPE_BASE ** (-(2.0 * np.arange(HALF, dtype=np.float64)) / H)
    angles = inverse[:, None] * np.arange(T, dtype=np.float64)[None, :]
    return np.cos(angles).astype(np.float32), np.sin(angles).astype(np.float32)


def parts_of(row):
    hi = row.astype(BF).astype(F32)
    rest = row - hi
    mid = rest.astype(BF).astype(F32)
    return [hi, mid, rest - mid]


def lane_tiles():
    return [slice(128 * i, 128 * i + 128) for i in range(T // 128)]


class Work:
    def __init__(self, order, refs):
        self.order = order
        self.__dict__.update(refs)

    def start(self):
        count = self.length[0]
        place = lax.broadcasted_iota(jnp.int32, (8, T), 1)
        valid = (place < count).astype(F32)
        self.valid[...] = valid
        for ts in lane_tiles():
            self.S[0, :, ts] = self.x[:, ts].astype(F32)
            self.G[:, ts] = jnp.where(valid[0:1, ts] > 0.0, self.ct[:, ts].astype(F32), 0.0)
        self.gainA[...] = jnp.broadcast_to(self.ga[...].reshape(1, D), (128, D)).T
        self.gainM[...] = jnp.broadcast_to(self.gm[...].reshape(1, D), (128, D)).T
        row = lax.broadcasted_iota(jnp.int32, (H, 1024), 0)
        lane = lax.broadcasted_iota(jnp.int32, (H, 1024), 1)
        self.pick[...] = jnp.where(lane == 128 * (row // 8) + 120 + lax.rem(row, 8), 1.0, 0.0).astype(BF)
        self.gacc[...] = jnp.zeros_like(self.gacc)
        def blank(h, carry):
            self.QA[0, h, H:, :] = jnp.zeros((H, T), BF)
            self.QA[1, h, H:, :] = jnp.zeros((H, T), BF)
            self.DOA[h, H:, :] = jnp.zeros((H, T), BF)
            return carry

        lax.fori_loop(0, NQ, blank, 0)

        def clear(i, carry):
            rows = pl.ds(pl.multiple_of(i * 64, 64), 64)
            self.DA[rows, :] = jnp.zeros((64, 1024), BF)
            self.DO[rows, :] = jnp.zeros((64, D), BF)
            self.DD[rows, :] = jnp.zeros((64, FF), BF)
            for k in range(3):
                self.DG[k, rows, :] = jnp.zeros((64, 1024), BF)
            return carry

        lax.fori_loop(0, D // 64, clear, 0)

    def norm(self, src, r, gain, dst, rho_ref, row):
        for ts in lane_tiles():
            v = src[r, :, ts]
            total = jnp.sum(v * v, axis=0, keepdims=True)
            if row is not None:
                self.stat[r, row : row + 1, ts] = total
            rho = lax.rsqrt(total * (1.0 / D) + EPS)
            rho_ref[r, 0:1, ts] = rho
            dst[r, :, ts] = (v * rho * gain[...]).astype(BF)

    def natural_rows(self, ref, base, width, first, count):
        pieces = []
        row = first
        while row < first + count:
            f, i = row // width, row % width
            n = min(width - i, first + count - row)
            at = 128 * self.order.index(f) + base + i
            pieces.append(ref[at : at + n, :])
            row += n
        return pieces[0] if len(pieces) == 1 else jnp.concatenate(pieces, axis=0)

    def prepare(self, r):
        self.norm(self.S, r, self.gainA, self.XA, self.rhoA, 0)

    def project(self, r):
        def part(c, carry):
            cs = pl.ds(pl.multiple_of(512 * c, 512), 512)
            self.Y[cs, :] = dot(self.WA[:, cs], self.XA[r], 0, 0)
            return carry

        for c in range(2):
            part(c, 0)
        cos, sin = self.cos[...], self.sin[...]
        one = jnp.ones((1, T), F32)
        place = lax.broadcasted_iota(jnp.int32, (1, T), 1)
        bias = jnp.where(place < self.length[0], 0.0, NEG)
        for h in range(NQ + NK):
            base, width, at = (0, QB, h) if h < NQ else (QB, KB, h - NQ)
            a = self.natural_rows(self.Y, base, width, H * at, HALF)
            b = self.natural_rows(self.Y, base, width, H * at + HALF, HALF)
            first, second = a * cos - b * sin, b * cos + a * sin
            if h < NQ:
                self.QA[r, h, 0:HALF, :] = (first * SCALE).astype(BF)
                self.QA[r, h, HALF:H, :] = (second * SCALE).astype(BF)
                self.QA[r, h, H : H + 16, :] = jnp.concatenate([one, jnp.zeros((15, T), F32)], axis=0).astype(BF)
            else:
                g = h - NQ
                key = jnp.concatenate([first, second], axis=0)
                self.KT[r, g] = key.astype(BF)
                v = jnp.concatenate(
                    [
                        self.natural_rows(self.Y, QB + KB, KB, H * g, HALF),
                        self.natural_rows(self.Y, QB + KB, KB, H * g + HALF, HALF),
                    ],
                    axis=0,
                )
                self.VT[g] = v.astype(BF)
                ones3 = jnp.ones((3, T), F32)
                tail = jnp.zeros((H - 4, T), F32)
                ktall = jnp.concatenate([key, bias, ones3, tail], axis=0)
                vtall = jnp.concatenate([v, jnp.zeros((1, T), F32), ones3, tail], axis=0)
                for ts in lane_tiles():
                    self.KTOK[r, g, ts, :] = ktall[:, ts].T.astype(BF)
                    self.VTOK[r, g, ts, :] = vtall[:, ts].T.astype(BF)

    def diagonal(self):
        key = lax.broadcasted_iota(jnp.int32, (BLK, BLK), 0)
        query = lax.broadcasted_iota(jnp.int32, (BLK, BLK), 1)
        return key <= query

    def attend(self, r, links):
        low, high = slice(0, BLK), slice(BLK, T)

        def head(h, carry):
            g = h // GROUP
            allowed = self.diagonal()
            at = pl.ds(pl.multiple_of(h * H, H), H)
            s = dot(self.KTOK[r, g, low, :], self.QA[r, h, :, low], 1, 0)
            s = jnp.where(allowed, s, NEG)
            top = jnp.max(s, axis=0, keepdims=True)
            p = jnp.exp(s - top)
            total = jnp.sum(p, axis=0, keepdims=True)
            o = dot(self.VT[g, :, low], p.astype(BF), 1, 0)
            self.AT[r, at, low] = (o * (1.0 / total)).astype(BF)
            lse0 = top + jnp.log(total)
            s0 = dot(self.KTOK[r, g, low, :], self.QA[r, h, :, high], 1, 0)
            s1 = dot(self.KTOK[r, g, high, :], self.QA[r, h, :, high], 1, 0)
            s1 = jnp.where(allowed, s1, NEG)
            top = jnp.maximum(jnp.max(s0, axis=0, keepdims=True), jnp.max(s1, axis=0, keepdims=True))
            p0 = jnp.exp(s0 - top)
            p1 = jnp.exp(s1 - top)
            total = jnp.sum(p0, axis=0, keepdims=True) + jnp.sum(p1, axis=0, keepdims=True)
            o = dot(self.VT[g, :, low], p0.astype(BF), 1, 0) + dot(self.VT[g, :, high], p1.astype(BF), 1, 0)
            self.AT[r, at, high] = (o * (1.0 / total)).astype(BF)
            lse1 = top + jnp.log(total)
            lse = jnp.concatenate([lse0, lse1], axis=1)
            rows = [jnp.ones((1, T), F32)] + parts_of(-lse) + [jnp.zeros((12, T), F32)]
            self.QA[r, h, H : H + 16, :] = jnp.concatenate(rows, axis=0).astype(BF)
            return carry

        def group(g, carry):
            lax.fori_loop(0, GROUP, lambda k, c: head(GROUP * g + k, c), 0, unroll=True)
            for k in range(NK):
                links.run_if((r == 0) & (g == k), HEADS[k])
            return carry

        lax.fori_loop(0, NK, group, 0)

    def rest_of_output(self):
        self.WO[:, NF * OW :] = dot(self.WA[...], self.pick[...], 1, 1).astype(BF)

    def after(self, value, src, r, dst, to, row, squares):
        n = value.shape[0]
        dst[to, row : row + n, :] = src[r, row : row + n, :] + value
        for i in range(n // 8):
            part = value[8 * i : 8 * i + 8]
            squares = squares + part * part
        return squares

    def out_project(self, r):
        self.Y[0:D, :] = dot(self.WO[...], self.AT[r], 0, 0)
        squares = jnp.zeros((8, T), F32)
        for b in range(NF):
            f = self.order[b]
            squares = self.after(self.Y[OW * b : OW * b + OW, :], self.S, r, self.M, r, QB * f, squares)
            at = NF * OW + 8 * b
            squares = self.after(self.Y[at : at + 8, :], self.S, r, self.M, r, QB * f + OW, squares)
        self.stat[r, 1:2, :] = jnp.sum(squares, axis=0, keepdims=True)

    def mlp(self, r, links):
        self.norm(self.M, r, self.gainM, self.XM, self.rhoM, None)

        def half(y, carry):
            cs = pl.ds(pl.multiple_of(512 * y, 512), 512)

            def part(i, carry):
                to = pl.ds(pl.multiple_of(512 * i, 512), 512)
                self.Y[to, :] = dot(self.WG[i, :, cs], self.XM[r], 0, 0)
                return carry

            for i in range(3):
                part(i, 0)

            def block(z, carry):
                f = self.natural(y, z)
                for j in range(3):
                    gate_at, up_at = self.places(j)
                    gate = self.Y[pl.ds(pl.multiple_of(gate_at[0] * 512 + 128 * z + gate_at[1], 64), 64), :]
                    up = self.Y[pl.ds(pl.multiple_of(up_at[0] * 512 + 128 * z + up_at[1], 64), 64), :]
                    rows = pl.ds(pl.multiple_of(FB * f + 64 * j, 64), 64)
                    self.GATE[r, rows, :] = gate.astype(BF)
                    self.UP[r, rows, :] = up.astype(BF)
                    self.HID[r, rows, :] = (gate * jax.nn.sigmoid(gate) * up).astype(BF)
                return carry

            for z in range(4):
                block(z, 0)
            links.run_if(r == 0, MLP[y])
            return carry

        for y in range(2):
            half(y, 0)
        self.Y[0:D, :] = dot(self.WDT[...], self.HID[r], 1, 0)
        squares = jnp.zeros((8, T), F32)
        for b in range(NF):
            squares = self.after(self.Y[QB * b : QB * b + QB, :], self.M, r, self.S, r + 1, QB * self.order[b], squares)
        self.stat[r, 2:3, :] = jnp.sum(squares, axis=0, keepdims=True)

    def natural(self, y, z):
        return 2 * z + y if self.order[1] == 2 else 4 * y + z

    def places(self, j):
        return ((0, 0), (0, 64), (1, 0))[j], ((1, 64), (2, 0), (2, 64))[j]

    def write_output(self):
        valid = self.valid[0:1, :]
        for ts in lane_tiles():
            v = jnp.where(valid[:, ts] > 0.0, self.S[2, :, ts], 0.0)
            self.out[:, ts] = v.astype(BF)

    def pack_down(self):
        for k in range(NF // 2):
            rows = [self.G[QB * self.order[b] : QB * self.order[b] + QB, :] for b in (2 * k, 2 * k + 1)]
            self.GLD[2 * QB * k : 2 * QB * k + 2 * QB, :] = jnp.concatenate(rows, axis=0).astype(BF)

    def pack_out(self):
        tails = []
        for b in range(NF):
            at = QB * self.order[b]
            self.GLO[OW * b : OW * b + OW, :] = self.G[at : at + OW, :].astype(BF)
            tails.append(self.G[at + OW : at + QB, :])
        self.GLO[NF * OW : D, :] = jnp.concatenate(tails, axis=0).astype(BF)

    def add_term(self, dst, index, value):
        dst[index] = (value + dst[index].astype(F32)).astype(dst.dtype)

    def norm_back(self, src, r, rho_ref, gain, slot):
        for ts in lane_tiles():
            e, v, rho = self.E[:, ts], src[r, :, ts], rho_ref[r, 0:1, ts]
            u = e * gain[...]
            mean = jnp.sum(u * v, axis=0, keepdims=True) * (1.0 / D)
            self.gacc[slot] += e * (v * rho)
            self.G[:, ts] = self.G[:, ts] + rho * (u - v * (rho * rho * mean))

    def mlp_back(self, r, links):
        self.pack_down()
        for c in range(2):
            cs = slice(768 * c, 768 * c + 768)
            self.add_term(self.DD, (slice(None), cs), dot(self.GLD[...], self.HID[r, cs, :], 1, 1))
        links.run_if(r == 0, AFTER_DOWN)

        def hidden(k, carry):
            rows = pl.ds(pl.multiple_of(2 * FB * k, 128), 2 * FB)
            self.Y[0 : 2 * FB, :] = dot(self.WDT[:, rows], self.GLD[...], 0, 0)
            for m in range(2):
                f = 2 * k + m
                b = k + 4 * m if self.order[1] == 2 else f
                for j in range(3):
                    at = pl.ds(pl.multiple_of(FB * f + 64 * j, 64), 64)
                    grad = self.Y[FB * m + 64 * j : FB * m + 64 * j + 64, :]
                    gate = self.GATE[r, at, :].astype(F32)
                    up = self.UP[r, at, :].astype(F32)
                    sig = jax.nn.sigmoid(gate)
                    silu = gate * sig
                    gate_at, up_at = self.places(j)
                    to = pl.ds(pl.multiple_of(1024 * gate_at[0] + 128 * b + gate_at[1], 64), 64)
                    self.DGU[to, :] = (grad * up * (sig + silu * (1.0 - sig))).astype(BF)
                    to = pl.ds(pl.multiple_of(1024 * up_at[0] + 128 * b + up_at[1], 64), 64)
                    self.DGU[to, :] = (grad * silu).astype(BF)
            links.run_if(r == 0, HIDDEN[k])
            return carry

        for k in range(4):
            hidden(k, 0)

        def matrix(i, carry):
            grad = self.DGU[pl.ds(pl.multiple_of(1024 * i, 1024), 1024), :]
            self.add_term(self.DG, (i,), dot(self.XM[r], grad, 1, 1))
            links.run_if(r == 0, AFTER_GATE[i])
            return carry

        for i in range(3):
            matrix(i, 0)
        self.E[...] = dot(self.WG[0], self.DGU[0:1024, :], 1, 0)

        def back(i, carry):
            grad = self.DGU[pl.ds(pl.multiple_of(1024 * i, 1024), 1024), :]
            self.E[...] = self.E[...] + dot(self.WG[i], grad, 1, 0)
            return carry

        for i in (1, 2):
            back(i, 0)
        links.run_if(r == 0, BEFORE_NORM)
        self.norm_back(self.M, r, self.rhoM, self.gainM, 1)

    def attend_back(self, r, links):
        self.pack_out()
        term = dot(self.AT[r], self.GLO[0:D, :], 1, 1)
        self.add_term(self.DO, (slice(None), slice(0, NF * OW)), term[:, : NF * OW])
        self.DO[:, NF * OW :] = term[:, NF * OW :].astype(BF)
        links.run_if(r == 0, AFTER_OUT)
        self.E[...] = dot(self.WO[...], self.GLO[0:D, :], 1, 0)
        links.run_if(r == 0, BEFORE_HEADS)
        for h in range(NQ):
            rows = slice(H * h, H * h + H)
            do = self.E[rows, :].astype(BF)
            self.DOA[h, 0:H, :] = do
            delta = jnp.sum(do.astype(F32) * self.AT[r, rows, :].astype(F32), axis=0, keepdims=True)
            rows = [jnp.zeros((1, T), F32)] + parts_of(-delta) + [jnp.zeros((12, T), F32)]
            self.DOA[h, H : H + 16, :] = jnp.concatenate(rows, axis=0).astype(BF)
        low, high = slice(0, BLK), slice(BLK, T)
        self.Y[D : D + 2 * NK * H, :] = jnp.zeros((2 * NK * H, T), F32)

        def head(h, carry):
            g = h // GROUP
            allowed = self.diagonal()
            at = pl.ds(pl.multiple_of(h * H, H), H)
            kat = pl.ds(pl.multiple_of(D + g * H, H), H)
            vat = pl.ds(pl.multiple_of(D + NK * H + g * H, H), H)
            q, do = self.QA[r, h], self.DOA[h]
            k0, k1 = self.KTOK[r, g, low, :], self.KTOK[r, g, high, :]
            v0, v1 = self.VTOK[r, g, low, :], self.VTOK[r, g, high, :]
            t0, t1 = self.KT[r, g, :, low], self.KT[r, g, :, high]

            p = jnp.where(allowed, jnp.exp(dot(k0, q[:, low], 1, 0)), 0.0)
            ds = (p * dot(v0, do[:, low], 1, 0)).astype(BF)
            p = p.astype(BF)
            self.Y[at, low] = dot(t0, ds, 1, 0) * SCALE
            dk0 = dot(q[0:H, low], ds, 1, 1)
            dv0 = dot(do[0:H, low], p, 1, 1)

            p = jnp.exp(dot(k0, q[:, high], 1, 0))
            ds = (p * dot(v0, do[:, high], 1, 0)).astype(BF)
            p = p.astype(BF)
            dq = dot(t0, ds, 1, 0)
            dk0 += dot(q[0:H, high], ds, 1, 1)
            dv0 += dot(do[0:H, high], p, 1, 1)

            p = jnp.where(allowed, jnp.exp(dot(k1, q[:, high], 1, 0)), 0.0)
            ds = (p * dot(v1, do[:, high], 1, 0)).astype(BF)
            p = p.astype(BF)
            self.Y[at, high] = (dq + dot(t1, ds, 1, 0)) * SCALE
            self.Y[kat, low] += dk0
            self.Y[vat, low] += dv0
            self.Y[kat, high] += dot(q[0:H, high], ds, 1, 1)
            self.Y[vat, high] += dot(do[0:H, high], p, 1, 1)
            return carry

        def group(g, carry):
            lax.fori_loop(0, GROUP, lambda k, c: head(GROUP * g + k, c), 0, unroll=True)
            for k in range(NK):
                links.run_if((r == 0) & (g == k), BACK_HEADS[k])
            return carry

        lax.fori_loop(0, NK, group, 0)

    def project_back(self, r, links):
        cos, sin = self.cos[...], self.sin[...]
        for h in range(NQ + NK):
            first, second = slice(H * h, H * h + HALF), slice(H * h + HALF, H * h + H)
            a, b = self.Y[first, :], self.Y[second, :]
            self.Y[first, :] = a * cos + b * sin
            self.Y[second, :] = b * cos - a * sin
        for b in range(NF):
            f = self.order[b]
            rows = jnp.concatenate(
                [
                    self.Y[QB * f : QB * f + QB, :],
                    self.Y[D + KB * f : D + KB * f + KB, :],
                    self.Y[D + NK * H + KB * f : D + NK * H + KB * f + KB, :],
                    jnp.zeros((128 - QB - 2 * KB, T), F32),
                ],
                axis=0,
            )
            self.GLO[128 * b : 128 * b + 128, :] = rows.astype(BF)
        def part(c, carry):
            cs = pl.ds(pl.multiple_of(512 * c, 512), 512)
            term = dot(self.XA[r], self.GLO[cs, :], 1, 1) + dot(self.DO[:, NF * OW :], self.pick[:, cs], 1, 0)
            self.add_term(self.DA, (slice(None), cs), term)
            return carry

        for c in range(2):
            part(c, 0)
        links.run_if(r == 0, AFTER_QKV)
        self.E[...] = dot(self.WA[...], self.GLO[...], 1, 0)
        self.norm_back(self.S, r, self.rhoA, self.gainA, 0)

    def write_grad(self):
        for ts in lane_tiles():
            self.gin[:, ts] = self.G[:, ts]

    def small(self):
        valid = self.valid[0:1, :]
        rows = [jnp.sum(self.gacc[i].T, axis=0, keepdims=True) for i in range(2)]
        sums = jnp.sum(jnp.where(valid > 0.0, jnp.concatenate([self.stat[0, 0:3], self.stat[1, 0:3]], axis=0), 0.0), axis=1, keepdims=True)
        count = jnp.sum(valid, axis=1, keepdims=True)
        lane = lax.broadcasted_iota(jnp.int32, (6, D), 1)
        return jnp.concatenate(rows + [jnp.where(lane < 128, sums, count)], axis=0)


SCRATCH = dict(
    S=((3, D, T), F32), G=((D, T), F32), E=((D, T), F32), Y=((1536, T), F32),
    XA=((2, D, T), BF), XM=((2, D, T), BF), rhoA=((2, 8, T), F32), rhoM=((2, 8, T), F32),
    QA=((2, NQ, 128, T), BF), KT=((2, NK, H, T), BF), VT=((NK, H, T), BF),
    KTOK=((2, NK, T, 128), BF), VTOK=((2, NK, T, 128), BF), AT=((2, D, T), BF), M=((2, D, T), F32),
    GATE=((2, FF, T), BF), UP=((2, FF, T), BF), HID=((2, FF, T), BF),
    GLD=((D, T), BF), GLO=((1024, T), BF), DGU=((2 * FF, T), BF), DOA=((NQ, 128, T), BF),
    stat=((2, 8, T), F32), valid=((8, T), F32), gacc=((2, D, 128), F32), gainA=((D, 128), F32), gainM=((D, 128), F32), pick=((H, 1024), BF),
)
WEIGHTS = dict(WA=((D, 1024), BF), WO=((D, D), BF), WG=((3, D, 1024), BF), WDT=((D, FF), BF))
GRADS = dict(DA=((D, 1024), BF), DO=((D, D), BF), DG=((3, D, 1024), BF), DD=((D, FF), BF))

class Alone:
    def run_if(self, condition, steps):
        pass


def applications(w, links):
    def forward(r, carry):
        w.prepare(r)
        links.run_if(r == 0, BEFORE_PROJECT)
        w.project(r)
        links.run_if(r == 0, AFTER_PROJECT)
        w.attend(r, links)
        pl.when(r == 0)(w.rest_of_output)
        links.run_if(r == 0, BEFORE_OUT)
        w.out_project(r)
        links.run_if(r == 0, BEFORE_MLP)
        w.mlp(r, links)
        return carry

    def backward(i, carry):
        w.mlp_back(1 - i, links)
        w.attend_back(1 - i, links)
        w.project_back(1 - i, links)
        return carry

    lax.fori_loop(0, 2, forward, 0)
    w.write_output()
    lax.fori_loop(0, 2, backward, 0)


def compute_kernel(order, names, *refs):
    w = Work(order, dict(zip(names, refs)))
    w.start()
    applications(w, Alone())
    w.write_grad()
    w.tiny[...] = w.small()


def local_compute(order, x, length, ga, gm, ct, packed):
    cos, sin = rope_tables()
    ins = dict(length=length, x=x, ct=ct, ga=ga, gm=gm, cos=jnp.asarray(cos), sin=jnp.asarray(sin), **packed)
    outs = dict(out=((D, T), BF), gin=((D, T), F32), tiny=((8, D), F32), **GRADS)
    names = list(ins) + list(outs) + list(SCRATCH)
    vmem = pl.BlockSpec(memory_space=pltpu.VMEM)
    results = pl.pallas_call(
        functools.partial(compute_kernel, order, names),
        out_shape=[jax.ShapeDtypeStruct(*s) for s in outs.values()],
        in_specs=[pl.BlockSpec(memory_space=pltpu.SMEM)] + [vmem] * (len(ins) - 1),
        out_specs=[vmem] * len(outs),
        scratch_shapes=[pltpu.VMEM(*s) for s in SCRATCH.values()],
        compiler_params=pltpu.CompilerParams(vmem_limit_bytes=VMEM_LIMIT),
    )(*ins.values())
    return dict(zip(outs, results))


def pack(order, q, k, v, o, g, u, d):
    def cols(w, width):
        return w.reshape(w.shape[0], NF, width)[:, np.array(order)]
    ob = cols(o, QB)
    wa = jnp.concatenate([cols(q, QB), cols(k, KB), cols(v, KB), ob[:, :, OW:]], axis=2).reshape(D, 1024)
    wo = jnp.concatenate([ob[:, :, :OW].reshape(D, NF * OW), ob[:, :, OW:].reshape(D, D - NF * OW)], axis=1)
    wg = jnp.concatenate([cols(g, FB), cols(u, FB)], axis=2).reshape(D, NF, 3, 128)
    wg = wg.transpose(2, 0, 1, 3).reshape(3, D, 1024)
    wd = d.T.reshape(NF, QB, FF)[np.array(order)].reshape(D, FF)
    return dict(WA=wa, WO=wo, WG=wg, WDT=wd)


def unpack(order, r):
    back = np.argsort(np.array(order))
    a = r["DA"].astype(F32).reshape(D, NF, 128)[:, back]
    o = r["DO"][:, : NF * OW].astype(F32).reshape(D, NF, OW)[:, back]
    o = jnp.concatenate([o, a[:, :, 120:]], axis=2).reshape(D, D)
    g = r["DG"].astype(F32).reshape(3, D, NF, 128).transpose(1, 2, 0, 3).reshape(D, NF, 2 * FB)[:, back]
    d = r["DD"].astype(F32).reshape(NF, QB, FF)[back].reshape(D, FF).T
    return (
        a[:, :, :QB].reshape(D, D), a[:, :, QB : QB + KB].reshape(D, NK * H), a[:, :, QB + KB : 120].reshape(D, NK * H),
        o, g[:, :, :FB].reshape(D, FF), g[:, :, FB:].reshape(D, FF), d,
    )


PIECES = ("A", "O", "G0", "G1", "G2", "D0", "D1")
DCUT = dict(D0=(0, 256), D1=(256, 128))
MESH = pl.DeviceIdType.MESH


def region(refs, piece, dp, y, z=0, count=4):
    ref, line = refs[piece[0]], 4 * y + z
    if piece[0] == "D":
        first, size = DCUT[piece]
        rows = pl.ds(pl.multiple_of(QB * line, 16), QB * count)
        return ref.at[rows, pl.ds(pl.multiple_of(LANES * dp + first, 128), size)]
    width = OW if piece == "O" else 128
    rows = pl.ds(pl.multiple_of(ROWS * dp, 16), ROWS)
    lanes = pl.ds(pl.multiple_of(width * line, 128), width * count)
    return ref.at[int(piece[1]), rows, lanes] if piece[0] == "G" else ref.at[rows, lanes]


def shape_of(piece, count):
    if piece[0] == "D":
        return (QB * count, DCUT[piece][1])
    return (ROWS, (OW if piece == "O" else 128) * count)


def slip_shape(piece):
    return (QB + 8, DCUT[piece][1]) if piece[0] == "D" else (ROWS, 128)


def cut(piece, line, z):
    if piece == "O":
        return jnp.concatenate([line[:, OW * z : OW * z + OW]] * 2, axis=1)
    return jnp.concatenate([line[QB * z : QB * z + QB], jnp.zeros((8, line.shape[1]), F32)], axis=0)


class Links:
    def __init__(self, refs):
        self.__dict__.update(refs)
        self.weights = dict(A=refs["WA"], O=refs["WO"], G=refs["WG"], D=refs["WDT"])
        self.grads = dict(A=refs["DA"], O=refs["DO"], G=refs["DG"], D=refs["DD"])
        self.dp, f = lax.axis_index("dp"), lax.axis_index("fsdp")
        self.x, self.c = self.dp // 2, lax.rem(self.dp, 2)
        self.z, self.y = f // 2, lax.rem(f, 2)
        self.ny = 1 - self.y
        self.theirs = [2 * i + 1 - self.c for i in range(2)]
        self.far = 2 * (1 - self.x) + self.c
        self.other = 2 * self.x + 1 - self.c
        self.sib = (self.other, f)
        self.xn = (self.far, f)
        self.yn = (self.dp, 2 * self.z + 1 - self.y)
        self.peer = [None] + [lax.rem(self.z + k, 4) for k in (1, 2, 3)]
        self.zn = [None] + [(self.dp, 2 * self.peer[k] + self.y) for k in (1, 2, 3)]
        self.copies = {}
        self.used = 0

    def greet(self):
        for device in [self.sib, self.xn, self.yn] + self.zn[1:]:
            pl.semaphore_signal(pltpu.get_barrier_semaphore(), inc=1, device_id=device, device_id_type=MESH)

    def met(self):
        pl.semaphore_wait(pltpu.get_barrier_semaphore(), 6)

    def send(self, name, src, dst, device):
        index = self.used
        self.used += 1

        def copy():
            return pltpu.make_async_remote_copy(
                src_ref=src(),
                dst_ref=dst(),
                send_sem=self.sent.at[index],
                recv_sem=self.came.at[index],
                device_id=device,
                device_id_type=MESH,
            )

        copy().start()
        self.copies[name] = copy

    def arrived(self, *names):
        for name in names:
            self.copies[name]().wait_recv()

    def finish(self):
        for copy in self.copies.values():
            copy().wait_send()

    def run_if(self, condition, steps):
        if steps:
            pl.when(condition)(functools.partial(self.run, *steps))

    def run(self, *steps):
        for step in steps:
            kind, piece = step.split()
            getattr(self, kind)(piece)


    def spread(self, tag, p, device, dp=None, y=None, z=0, count=4):
        block = lambda: region(self.weights, p, self.dp if dp is None else dp, self.y if y is None else y, z, count)
        self.send(("w", p, tag), block, block, device)

    def share(self, p):
        for k in (1, 3, 2):
            if p[0] in "OD":
                block = lambda: getattr(self, "slip" + p).at[self.z]
                self.send(("w", p, f"z{k}"), block, block, self.zn[k])
            else:
                self.spread(f"z{k}", p, self.zn[k], z=self.z, count=1)

    def line(self, p):
        self.arrived(*[("w", p, f"z{k}") for k in (1, 2, 3)])
        if p[0] in "OD":
            slips = [getattr(self, "slip" + p)[z].astype(F32) for z in range(4)]
            if p == "O":
                whole = jnp.concatenate([slip[:, :OW] for slip in slips], axis=1)
            else:
                whole = jnp.concatenate([slip[:QB] for slip in slips], axis=0)
            region(self.weights, p, self.dp, self.y)[...] = whole.astype(BF)
        self.spread("x", p, self.xn)
        self.spread("y", p, self.yn)
        self.spread("s", p, self.sib)

    def cross(self, p):
        self.arrived(("w", p, "x"))
        self.spread("xy", p, self.yn, dp=self.far, count=2)
        self.spread("sx", p, self.sib, dp=self.far)
        self.arrived(("w", p, "y"))
        self.spread("yx", p, self.xn, y=self.ny, z=2, count=2)
        self.spread("sy", p, self.sib, y=self.ny)

    def rest(self, p):
        self.arrived(("w", p, "xy"))
        self.spread("sxy", p, self.sib, dp=self.far, y=self.ny, count=2)
        self.arrived(("w", p, "yx"))
        self.spread("syx", p, self.sib, dp=self.far, y=self.ny, z=2, count=2)

    def end(self, p):
        self.arrived(*[("w", p, tag) for tag in ("s", "sx", "sy", "sxy", "syx")])


    def term(self, p, dp, y, z=0, count=4):
        return region(self.grads, p, dp, y, z, count)

    def add(self, p, dp, y, z, count, came):
        at = self.term(p, dp, y, z, count)
        at[...] = at[...] + came[...]

    def sibs(self, p):
        room = getattr(self, "one" + p)
        for i in range(2):
            for y in range(2):
                dp = self.theirs[i]
                self.send(
                    ("g", p, "s", i, y),
                    lambda dp=dp, y=y: self.term(p, dp, y),
                    lambda i=i, y=y: room.at[i, y],
                    self.sib,
                )

    def pair(self, p):
        room = getattr(self, "one" + p)
        for i in range(2):
            for y in range(2):
                self.arrived(("g", p, "s", i, y))
                self.add(p, 2 * i + self.c, y, 0, 4, room.at[i, y])
        ups, across = getattr(self, "twoy" + p), getattr(self, "twox" + p)
        for i, dp in enumerate((self.dp, self.far)):
            self.send(
                ("g", p, "y", i), lambda dp=dp: self.term(p, dp, self.ny, 0, 2), lambda i=i: ups.at[i], self.yn
            )
        for j, y in enumerate((self.y, self.ny)):
            self.send(
                ("g", p, "x", j), lambda y=y: self.term(p, self.far, y, 2, 2), lambda j=j: across.at[j], self.xn
            )

    def twos(self, p):
        ups, across = getattr(self, "twoy" + p), getattr(self, "twox" + p)
        for i in (1, 0):
            self.arrived(("g", p, "y", i))
            self.add(p, (self.dp, self.far)[i], self.y, 0, 2, ups.at[i])
            if i == 1:
                self.send(
                    ("g", p, "yx"), lambda: self.term(p, self.far, self.y, 0, 2), lambda: getattr(self, "threex" + p), self.xn
                )
        for j in (1, 0):
            self.arrived(("g", p, "x", j))
            self.add(p, self.dp, (self.y, self.ny)[j], 2, 2, across.at[j])
            if j == 1:
                self.send(
                    ("g", p, "xy"), lambda: self.term(p, self.dp, self.ny, 2, 2), lambda: getattr(self, "threey" + p), self.yn
                )

    def fours(self, p):
        self.arrived(("g", p, "yx"))
        self.add(p, self.dp, self.y, 0, 2, getattr(self, "threex" + p))
        self.arrived(("g", p, "xy"))
        self.add(p, self.dp, self.y, 2, 2, getattr(self, "threey" + p))
        if p[0] in "OD":
            line = self.term(p, self.dp, self.y)[...].astype(F32)
            for z in range(4):
                getattr(self, "part" + p)[z] = cut(p, line, z).astype(BF)
        for k in (1, 3, 2):
            if p[0] in "OD":
                src = lambda k=k: getattr(self, "part" + p).at[self.peer[k]]
            else:
                src = lambda k=k: self.term(p, self.dp, self.y, self.peer[k], 1)
            self.send(("g", p, "z", k), src, lambda k=k: getattr(self, "four" + p).at[k - 1], self.zn[k])

    def total(self, p):
        own = getattr(self, "part" + p)[self.z] if p[0] in "OD" else self.term(p, self.dp, self.y, self.z, 1)[...]
        total = own.astype(F32)
        for k in (1, 2, 3):
            self.arrived(("g", p, "z", k))
            total = total + getattr(self, "four" + p)[k - 1].astype(F32)
        if p[0] == "D":
            first, size = DCUT[p]
            self.sumD[:, first : first + size] = total[:QB, :]
        else:
            at = 128 * ("A", "O", "G0", "G1", "G2").index(p)
            self.sumN[:, at : at + 128] = total


    def tiny(self, step):
        step = int(step)
        if step > 0:
            self.arrived(("t", step - 1))
            self.tinies[step] = self.tinies[step - 1] + self.tinyin[step - 1]
        if step < 3:
            device = (self.sib, self.xn, self.yn)[step]
            self.send(("t", step), lambda: self.tinies.at[step], lambda: self.tinyin.at[step], device)
        else:
            for k in (1, 2, 3):
                self.send(("t", step, k), lambda: self.tinies.at[3], lambda k=k: self.tinyz.at[k], self.zn[k])

    def tiny_end(self):
        self.tinyz[0] = self.tinies[3]
        for k in (1, 2, 3):
            self.arrived(("t", 3, k))
        total = None
        for z in range(4):
            term = self.tinyz[lax.rem(self.z - z + 4, 4)]
            total = term if total is None else total + term
        self.sumT[...] = total


def rooms():
    shapes = {}
    for p in PIECES:
        shapes["one" + p] = ((2, 2) + shape_of(p, 4), BF)
        for room in ("twoy", "twox"):
            shapes[room + p] = ((2,) + shape_of(p, 2), BF)
        for room in ("threex", "threey"):
            shapes[room + p] = (shape_of(p, 2), BF)
        shapes["four" + p] = ((3,) + slip_shape(p), BF)
        if p[0] in "OD":
            shapes["slip" + p] = ((4,) + slip_shape(p), BF)
            shapes["part" + p] = ((4,) + slip_shape(p), BF)
    shapes["tinies"] = ((4, 8, D), F32)
    shapes["tinyin"] = ((3, 8, D), F32)
    shapes["tinyz"] = ((4, 8, D), F32)
    return shapes


COPIES = len(PIECES) * (12 + 13) + 6


def pack_own(links, refs):
    rows = lambda *names: [refs[n][...].astype(F32) for n in names]
    q, k, v, o, g, u, d = rows("q", "k", "v", "o", "g", "u", "d")
    gu = jnp.concatenate([g, u], axis=1)
    whole = dict(A=jnp.concatenate([q, k.T, v.T, o[:, OW:]], axis=1), G0=gu[:, :128], G1=gu[:, 128:256], G2=gu[:, 256:])
    for p in PIECES:
        if p == "O":
            links.slipO[links.z] = cut(p, o, 0).astype(BF)
        elif p[0] == "D":
            first, size = DCUT[p]
            getattr(links, "slip" + p)[links.z] = cut(p, d[:, first : first + size], 0).astype(BF)
        else:
            region(links.weights, p, links.dp, links.y, links.z, 1)[...] = whole[p].astype(BF)


BEGIN = ("share A", "share O", "share G0", "share G1", "share G2", "share D0", "share D1")
BEFORE_PROJECT = ("line A", "line O", "cross A", "line G0", "cross O", "rest A", "line G1", "end A")
AFTER_PROJECT = ("cross G0", "rest O", "line G2")
HEADS = (("cross G1", "rest G0"), ("line D0",), ("cross G2", "rest G1"))
BEFORE_OUT = ("end O", "line D1")
BEFORE_MLP = ("cross D0", "rest G2", "end G0", "end G1", "end G2")
MLP = (("cross D1", "rest D0"), ("rest D1", "end D0", "end D1"))
AFTER_DOWN = ("sibs D0", "sibs D1")
HIDDEN = (("pair D0",), ("pair D1",), (), ("twos D0",))
AFTER_GATE = (("sibs G0", "twos D1"), ("sibs G1", "pair G0", "fours D0"), ("sibs G2", "pair G1", "fours D1"))
BEFORE_NORM = ("pair G2",)
AFTER_OUT = ("sibs O", "twos G0")
BEFORE_HEADS = ("pair O",)
BACK_HEADS = (("twos G1", "fours G0"), ("twos G2", "fours G1"), ("twos O", "fours G2"))
AFTER_QKV = ("sibs A", "fours O")
LAST = ("tiny 0", "pair A", "tiny 1", "twos A", "tiny 2")
VERY_LAST = ("total D0", "total D1", "total G0", "total G1", "total G2", "fours A", "tiny 3", "total O", "total A")


def whole_kernel(order, names, *args):
    refs = dict(zip(names, args))
    w, links = Work(order, refs), Links(refs)
    links.greet()
    pack_own(links, refs)
    links.met()
    links.run(*BEGIN)
    w.start()
    applications(w, links)
    links.tinies[0] = w.small()
    links.run(*LAST)
    w.write_grad()
    links.run(*VERY_LAST)
    links.tiny_end()
    links.finish()


def finish_kernel(*refs):
    out, gin, sums, sumd, tiny, oout, ogin, ga, q, k, v, o, gm, g, u, d, rms = refs
    oout[...] = out[...]
    ogin[...] = gin[...]
    q[...] = sums[:, :QB]
    k[...] = sums[:, QB : QB + KB].T
    v[...] = sums[:, QB + KB : 120].T
    o[...] = jnp.concatenate([sums[:, 128 : 128 + OW], sums[:, 120:128]], axis=1)
    g[...] = sums[:, 256 : 256 + FB]
    u[...] = sums[:, 256 + FB : 256 + 2 * FB]
    d[...] = sumd[...]
    ga[...] = tiny[0:1, :].reshape(D)
    gm[...] = tiny[1:2, :].reshape(D)
    lane = lax.broadcasted_iota(jnp.int32, (1, 3), 1)
    for r in range(2):
        first, second, third = [tiny[2 + 3 * r + i : 3 + 3 * r + i, 0:3] for i in range(3)]
        squares = jnp.where(lane == 0, first, jnp.where(lane == 1, second, third))
        rms[r : r + 1, :] = jnp.sqrt(squares / (tiny[2:3, 128:131] * D))


def whole(x, length, ga, q, k, v, o, gm, g, u, d, ct):
    order = [2 * (b % 4) + b // 4 for b in range(NF)]
    cos, sin = rope_tables()
    ins = dict(
        length=length, x=x[0].T, ct=ct[0].T, ga=ga, gm=gm, cos=jnp.asarray(cos), sin=jnp.asarray(sin),
        q=q, k=k.T, v=v.T, o=o, g=g, u=u, d=d.T,
    )
    outs = dict(
        out=((D, T), BF), gin=((D, T), F32), sumN=((ROWS, 256 + 2 * FB), F32), sumD=((QB, LANES), F32), sumT=((8, D), F32)
    )
    scratch = dict(SCRATCH, **WEIGHTS, **GRADS, **rooms())
    names = list(ins) + list(outs) + list(scratch) + ["sent", "came"]
    vmem = pl.BlockSpec(memory_space=pltpu.VMEM)
    r = pl.pallas_call(
        functools.partial(whole_kernel, order, names),
        out_shape=[jax.ShapeDtypeStruct(*s) for s in outs.values()],
        in_specs=[pl.BlockSpec(memory_space=pltpu.SMEM)] + [vmem] * (len(ins) - 1),
        out_specs=[vmem] * len(outs),
        scratch_shapes=[pltpu.VMEM(*s) for s in scratch.values()]
        + [pltpu.SemaphoreType.DMA((COPIES,)), pltpu.SemaphoreType.DMA((COPIES,))],
        compiler_params=pltpu.CompilerParams(
            vmem_limit_bytes=VMEM_LIMIT, collective_id=0, has_side_effects=True
        ),
    )(*ins.values())
    rows = [
        ((D, T), BF), ((D, T), F32), ((D,), F32), (q.shape, F32), (k.shape[::-1], F32), (v.shape[::-1], F32),
        (o.shape, F32), ((D,), F32), (g.shape, F32), (u.shape, F32), (d.shape[::-1], F32), ((2, 3), F32),
    ]
    out, gin, ga, q, k, v, o, gm, g, u, d, rms = pl.pallas_call(
        finish_kernel,
        out_shape=[jax.ShapeDtypeStruct(*s) for s in rows],
        in_specs=[vmem] * len(outs),
        out_specs=[vmem] * len(rows),
    )(*r)
    return out.T[None], gin.T[None], ga, q, k.T, v.T, o, gm, g, u, d.T, rms


def by_collectives(x, length, ga, q, k, v, o, gm, g, u, d, ct):
    order = list(range(NF))
    full = [lax.all_gather(lax.all_gather(w, "fsdp", axis=1, tiled=True), "dp", axis=0, tiled=True) for w in (q, k, v, o, g, u, d)]
    packed = pack(order, *full)
    results = [local_compute(order, x[i].T, length[i : i + 1], ga, gm, ct[i].T, packed) for i in range(x.shape[0])]
    out = jnp.stack([r["out"].T for r in results])
    gin = jnp.stack([r["gin"].T for r in results])
    tiny = lax.psum(sum(r["tiny"] for r in results), ("dp", "fsdp"))
    terms = [unpack(order, r) for r in results]
    grads = [
        lax.psum_scatter(
            lax.psum_scatter(sum(t), "dp", scatter_dimension=0, tiled=True), "fsdp", scatter_dimension=1, tiled=True
        )
        for t in zip(*terms)
    ]
    rms = jnp.sqrt(tiny[2:8, 0].reshape(2, 3) / (tiny[2, 128] * D))
    gq, gk, gv, go, gg, gu, gd = grads
    return out, gin, tiny[0], gq, gk, gv, go, tiny[1], gg, gu, gd, rms


def solution(mesh):
    blocks = P("dp", "fsdp")
    slots = P(("dp", "fsdp"), None, None)
    in_specs = (slots, P(("dp", "fsdp")), P(), blocks, blocks, blocks, blocks, P(), blocks, blocks, blocks, slots)
    out_specs = (slots, slots, P(), blocks, blocks, blocks, blocks, P(), blocks, blocks, blocks, P())

    def on_device(*args):
        fits = mesh.shape["dp"] == 4 and mesh.shape["fsdp"] == 8 and args[0].shape[0] == 1
        return (whole if fits else by_collectives)(*args)

    return jax.shard_map(on_device, mesh=mesh, in_specs=in_specs, out_specs=out_specs, check_vma=False)
```

profile of v0, /device:TPU:0, one launch (start us, length us, event | category | flops | bytes accessed | tf_op | source)
XLA Modules:
  0.0 138.5 jit_solution(11757445073636135170)
XLA Ops:
  1.3 133.8 %shard_map.229 = (bf16[576,512]{1,0:T(8,128)(2,1)}, f32[576,512]{1,0:T(8,128)}, f32[144,640]{1,0:T(8,128)}, f32[72,384]{1,0:T(8,128)}, f32[8,576]{1,0:T(8,128)}) custom-call(s32[1]{0:T(128)S(6)} %copy.26.args_0_, bf16[576,512]{1,0:T(8,128)(2,1)} %bitcast.18, bf16[576,512]{1,0:T(8,128)(2,1)} %bitcast.19, f32[576]{0:T(1024)} %args_3_.4, f32[576]{0:T(1024)} %args_4_.4, ...), custom_call_target="tpu_custom_call" | custom-call | tf_op jit(solution)/shard_map/pallas_call | solution.py:894
  135.1 3.3 %shard_map.230 = (bf16[576,512]{1,0:T(8,128)(2,1)}, f32[576,512]{1,0:T(8,128)}, f32[576]{0:T(1024)}, f32[144,72]{1,0:T(8,128)}, f32[24,144]{1,0:T(8,128)}, /*ind...) custom-call(bf16[576,512]{1,0:T(8,128)(2,1)} %get-tuple-element.29.r, ...), custom_call_target="tpu_custom_call" | custom-call | tf_op jit(solution)/shard_map/pallas_call | solution.py:909
where the time goes:
time: 139 us; the launch traced here: 138 us
  Pallas kernels  137 us (99%)
  between operations  1.4 us (1%)
    pallas_call x1, Pallas kernels, whole(): pl.pallas_call(functools.partial(whole_kernel, order, names), out_shape=[...  134 us
    pallas_call x1, Pallas kernels, whole(): pl.pallas_call(finish_kernel, out_shape=[jax.ShapeDtypeStruct(*s) for s i...  3.31 us

commit v1 on v0

--- a/solution.py
+++ b/solution.py
@@ -192,12 +192,12 @@
             return carry
 
         def group(g, carry):
-            lax.fori_loop(0, GROUP, lambda k, c: head(GROUP * g + k, c), 0, unroll=True)
-            for k in range(NK):
-                links.run_if((r == 0) & (g == k), HEADS[k])
-            return carry
-
-        lax.fori_loop(0, NK, group, 0)
+            [head(GROUP * g + k, 0) for k in range(GROUP)]
+            links.run_if(r == 0, HEADS[g])
+            return carry
+
+        for g in range(NK):
+            group(g, 0)
 
     def rest_of_output(self):
         self.WO[:, NF * OW :] = dot(self.WA[...], self.pick[...], 1, 1).astype(BF)
@@ -400,12 +400,12 @@
             return carry
 
         def group(g, carry):
-            lax.fori_loop(0, GROUP, lambda k, c: head(GROUP * g + k, c), 0, unroll=True)
-            for k in range(NK):
-                links.run_if((r == 0) & (g == k), BACK_HEADS[k])
-            return carry
-
-        lax.fori_loop(0, NK, group, 0)
+            [head(GROUP * g + k, 0) for k in range(GROUP)]
+            links.run_if(r == 0, BACK_HEADS[g])
+            return carry
+
+        for g in range(NK):
+            group(g, 0)
 
     def project_back(self, r, links):
         cos, sin = self.cos[...], self.sin[...]
@@ -543,31 +543,32 @@
     )
 
 
-PIECES = ("A", "O", "G0", "G1", "G2", "D0", "D1")
-DCUT = dict(D0=(0, 256), D1=(256, 128))
+PIECES = ("A0", "A1", "O", "G0", "G1", "G2", "D0", "D1")
+CUT = dict(A0=(0, 80), A1=(80, ROWS - 80), D0=(0, 256), D1=(256, 128))
 MESH = pl.DeviceIdType.MESH
 
 
 def region(refs, piece, dp, y, z=0, count=4):
     ref, line = refs[piece[0]], 4 * y + z
     if piece[0] == "D":
-        first, size = DCUT[piece]
+        first, size = CUT[piece]
         rows = pl.ds(pl.multiple_of(QB * line, 16), QB * count)
         return ref.at[rows, pl.ds(pl.multiple_of(LANES * dp + first, 128), size)]
     width = OW if piece == "O" else 128
-    rows = pl.ds(pl.multiple_of(ROWS * dp, 16), ROWS)
+    first, size = CUT.get(piece, (0, ROWS))
+    rows = pl.ds(pl.multiple_of(ROWS * dp + first, 16), size)
     lanes = pl.ds(pl.multiple_of(width * line, 128), width * count)
     return ref.at[int(piece[1]), rows, lanes] if piece[0] == "G" else ref.at[rows, lanes]
 
 
 def shape_of(piece, count):
     if piece[0] == "D":
-        return (QB * count, DCUT[piece][1])
-    return (ROWS, (OW if piece == "O" else 128) * count)
+        return (QB * count, CUT[piece][1])
+    return (CUT.get(piece, (0, ROWS))[1], (OW if piece == "O" else 128) * count)
 
 
 def slip_shape(piece):
-    return (QB + 8, DCUT[piece][1]) if piece[0] == "D" else (ROWS, 128)
+    return (QB + 8, CUT[piece][1]) if piece[0] == "D" else (CUT.get(piece, (0, ROWS))[1], 128)
 
 
 def cut(piece, line, z):
@@ -585,7 +586,9 @@
         self.x, self.c = self.dp // 2, lax.rem(self.dp, 2)
         self.z, self.y = f // 2, lax.rem(f, 2)
         self.ny = 1 - self.y
-        self.theirs = [2 * i + 1 - self.c for i in range(2)]
+        places = [(1 - self.x, self.ny), (self.x, self.ny), (1 - self.x, self.y), (self.x, self.y)]
+        self.mine = [(2 * x + self.c, y) for x, y in places]
+        self.theirs = [(2 * x + 1 - self.c, y) for x, y in places]
         self.far = 2 * (1 - self.x) + self.c
         self.other = 2 * self.x + 1 - self.c
         self.sib = (self.other, f)
@@ -689,55 +692,36 @@
         at[...] = at[...] + came[...]
 
     def sibs(self, p):
-        room = getattr(self, "one" + p)
-        for i in range(2):
-            for y in range(2):
-                dp = self.theirs[i]
-                self.send(
-                    ("g", p, "s", i, y),
-                    lambda dp=dp, y=y: self.term(p, dp, y),
-                    lambda i=i, y=y: room.at[i, y],
-                    self.sib,
-                )
+        for i in range(4):
+            src = lambda i=i: self.term(p, *self.theirs[i])
+            self.send(("g", p, "s", i), src, lambda i=i: getattr(self, "one" + p).at[i], self.sib)
 
     def pair(self, p):
-        room = getattr(self, "one" + p)
-        for i in range(2):
-            for y in range(2):
-                self.arrived(("g", p, "s", i, y))
-                self.add(p, 2 * i + self.c, y, 0, 4, room.at[i, y])
-        ups, across = getattr(self, "twoy" + p), getattr(self, "twox" + p)
-        for i, dp in enumerate((self.dp, self.far)):
-            self.send(
-                ("g", p, "y", i), lambda dp=dp: self.term(p, dp, self.ny, 0, 2), lambda i=i: ups.at[i], self.yn
-            )
-        for j, y in enumerate((self.y, self.ny)):
-            self.send(
-                ("g", p, "x", j), lambda y=y: self.term(p, self.far, y, 2, 2), lambda j=j: across.at[j], self.xn
-            )
+        for i in range(4):
+            self.arrived(("g", p, "s", i))
+            self.add(p, *self.mine[i], 0, 4, getattr(self, "one" + p).at[i])
+            if i < 2:
+                src = lambda i=i: self.term(p, *self.mine[i], 0, 2)
+                self.send(("g", p, "y", i), src, lambda i=i: getattr(self, "twoy" + p).at[i], self.yn)
+            if i in (0, 2):
+                src = lambda i=i: self.term(p, *self.mine[i], 2, 2)
+                self.send(("g", p, "x", i // 2), src, lambda i=i: getattr(self, "twox" + p).at[i // 2], self.xn)
 
     def twos(self, p):
-        ups, across = getattr(self, "twoy" + p), getattr(self, "twox" + p)
-        for i in (1, 0):
-            self.arrived(("g", p, "y", i))
-            self.add(p, (self.dp, self.far)[i], self.y, 0, 2, ups.at[i])
-            if i == 1:
-                self.send(
-                    ("g", p, "yx"), lambda: self.term(p, self.far, self.y, 0, 2), lambda: getattr(self, "threex" + p), self.xn
-                )
-        for j in (1, 0):
-            self.arrived(("g", p, "x", j))
-            self.add(p, self.dp, (self.y, self.ny)[j], 2, 2, across.at[j])
-            if j == 1:
-                self.send(
-                    ("g", p, "xy"), lambda: self.term(p, self.dp, self.ny, 2, 2), lambda: getattr(self, "threey" + p), self.yn
-                )
+        self.arrived(("g", p, "y", 0))
+        self.add(p, self.far, self.y, 0, 2, getattr(self, "twoy" + p).at[0])
+        src = lambda: self.term(p, self.far, self.y, 0, 2)
+        self.send(("g", p, "yx"), src, lambda: getattr(self, "threex" + p), self.xn)
+        self.arrived(("g", p, "x", 0))
+        self.add(p, self.dp, self.ny, 2, 2, getattr(self, "twox" + p).at[0])
+        src = lambda: self.term(p, self.dp, self.ny, 2, 2)
+        self.send(("g", p, "xy"), src, lambda: getattr(self, "threey" + p), self.yn)
 
     def fours(self, p):
-        self.arrived(("g", p, "yx"))
-        self.add(p, self.dp, self.y, 0, 2, getattr(self, "threex" + p))
-        self.arrived(("g", p, "xy"))
-        self.add(p, self.dp, self.y, 2, 2, getattr(self, "threey" + p))
+        self.arrived(("g", p, "y", 1), ("g", p, "x", 1), ("g", p, "yx"), ("g", p, "xy"))
+        for z, two, three in ((0, "twoy", "threex"), (2, "twox", "threey")):
+            at = self.term(p, self.dp, self.y, z, 2)
+            at[...] = at[...] + getattr(self, two + p)[1] + getattr(self, three + p)[...]
         if p[0] in "OD":
             line = self.term(p, self.dp, self.y)[...].astype(F32)
             for z in range(4):
@@ -756,11 +740,12 @@
             self.arrived(("g", p, "z", k))
             total = total + getattr(self, "four" + p)[k - 1].astype(F32)
         if p[0] == "D":
-            first, size = DCUT[p]
+            first, size = CUT[p]
             self.sumD[:, first : first + size] = total[:QB, :]
         else:
-            at = 128 * ("A", "O", "G0", "G1", "G2").index(p)
-            self.sumN[:, at : at + 128] = total
+            at = 128 * ("A", "O", "G0", "G1", "G2").index("A" if p[0] == "A" else p)
+            first, size = CUT.get(p, (0, ROWS))
+            self.sumN[first : first + size, at : at + 128] = total
 
 
     def tiny(self, step):
@@ -789,7 +774,7 @@
 def rooms():
     shapes = {}
     for p in PIECES:
-        shapes["one" + p] = ((2, 2) + shape_of(p, 4), BF)
+        shapes["one" + p] = ((4,) + shape_of(p, 4), BF)
         for room in ("twoy", "twox"):
             shapes[room + p] = ((2,) + shape_of(p, 2), BF)
         for room in ("threex", "threey"):
@@ -811,34 +796,40 @@
     rows = lambda *names: [refs[n][...].astype(F32) for n in names]
     q, k, v, o, g, u, d = rows("q", "k", "v", "o", "g", "u", "d")
     gu = jnp.concatenate([g, u], axis=1)
-    whole = dict(A=jnp.concatenate([q, k.T, v.T, o[:, OW:]], axis=1), G0=gu[:, :128], G1=gu[:, 128:256], G2=gu[:, 256:])
+    a = jnp.concatenate([q, k.T, v.T, o[:, OW:]], axis=1)
+    whole = dict(A0=a[:80], A1=a[80:], G0=gu[:, :128], G1=gu[:, 128:256], G2=gu[:, 256:])
     for p in PIECES:
         if p == "O":
             links.slipO[links.z] = cut(p, o, 0).astype(BF)
         elif p[0] == "D":
-            first, size = DCUT[p]
+            first, size = CUT[p]
             getattr(links, "slip" + p)[links.z] = cut(p, d[:, first : first + size], 0).astype(BF)
         else:
             region(links.weights, p, links.dp, links.y, links.z, 1)[...] = whole[p].astype(BF)
 
 
-BEGIN = ("share A", "share O", "share G0", "share G1", "share G2", "share D0", "share D1")
-BEFORE_PROJECT = ("line A", "line O", "cross A", "line G0", "cross O", "rest A", "line G1", "end A")
-AFTER_PROJECT = ("cross G0", "rest O", "line G2")
-HEADS = (("cross G1", "rest G0"), ("line D0",), ("cross G2", "rest G1"))
-BEFORE_OUT = ("end O", "line D1")
-BEFORE_MLP = ("cross D0", "rest G2", "end G0", "end G1", "end G2")
+BEGIN = ("share A0", "share A1", "share O", "share G0", "share G1", "share G2", "share D0", "share D1")
+BEFORE_PROJECT = (
+    "line A0", "line A1", "cross A0", "line O", "cross A1", "line G0", "rest A0", "cross O", "line G1", "rest A1", "line G2",
+    "end A0", "end A1",
+)
+AFTER_PROJECT = ("cross G0", "rest O")
+HEADS = (("line D0", "cross G1"), ("rest G0", "line D1"), ("end O", "cross G2"))
+BEFORE_OUT = ()
+BEFORE_MLP = ("rest G1", "cross D0", "rest G2", "end G0", "end G1", "end G2")
 MLP = (("cross D1", "rest D0"), ("rest D1", "end D0", "end D1"))
-AFTER_DOWN = ("sibs D0", "sibs D1")
-HIDDEN = (("pair D0",), ("pair D1",), (), ("twos D0",))
-AFTER_GATE = (("sibs G0", "twos D1"), ("sibs G1", "pair G0", "fours D0"), ("sibs G2", "pair G1", "fours D1"))
-BEFORE_NORM = ("pair G2",)
-AFTER_OUT = ("sibs O", "twos G0")
-BEFORE_HEADS = ("pair O",)
-BACK_HEADS = (("twos G1", "fours G0"), ("twos G2", "fours G1"), ("twos O", "fours G2"))
-AFTER_QKV = ("sibs A", "fours O")
-LAST = ("tiny 0", "pair A", "tiny 1", "twos A", "tiny 2")
-VERY_LAST = ("total D0", "total D1", "total G0", "total G1", "total G2", "fours A", "tiny 3", "total O", "total A")
+AFTER_DOWN = ("sibs D1", "sibs D0")
+HIDDEN = (("pair D1",), ("pair D0",), (), ())
+AFTER_GATE = (("sibs G0", "twos D1"), ("sibs G1",), ("pair G0", "sibs G2", "twos D0"))
+BEFORE_NORM = ("pair G1", "twos G0")
+AFTER_OUT = ("sibs O", "pair G2")
+BEFORE_HEADS = ("fours D1",)
+BACK_HEADS = (("twos G1", "pair O"), ("fours D0", "twos G2"), ("fours G0", "twos O"))
+AFTER_QKV = ("sibs A0", "sibs A1", "fours G1", "pair A0", "pair A1")
+LAST = (
+    "tiny 0", "fours G2", "fours O", "tiny 1", "total D1", "total D0", "twos A0", "tiny 2", "twos A1", "total G0",
+)
+VERY_LAST = ("fours A0", "total G1", "tiny 3", "total G2", "total O", "fours A1", "total A0", "total A1")
 
 
 def whole_kernel(order, names, *args):

time: 139 us -> 134 us (0.964)
  Pallas kernels: 137 us -> 132 us
    pallas_call x1, Pallas kernels: 134 us -> 129 us  [whole(): pl.pallas_call(functools.partial(whole_kernel, order, names), out_shape=[...]
where the time goes in v1:
time: 134 us
  Pallas kernels  132 us (99%)
  between operations  1.4 us (1%)
    pallas_call x1, Pallas kernels, whole(): pl.pallas_call(functools.partial(whole_kernel, order, names), out_shape=[...  129 us
    pallas_call x1, Pallas kernels, whole(): pl.pallas_call(finish_kernel, out_shape=[jax.ShapeDtypeStruct(*s) for s i...  3.31 us

profile of v1, /device:TPU:0, one launch (start us, length us, event | category | flops | bytes accessed | tf_op | source)
XLA Modules:
  0.0 133.6 jit_solution(18071613254466544986)
XLA Ops:
  1.3 128.9 %shard_map.229 = (bf16[576,512]{1,0:T(8,128)(2,1)}, f32[576,512]{1,0:T(8,128)}, f32[144,640]{1,0:T(8,128)}, f32[72,384]{1,0:T(8,128)}, f32[8,576]{1,0:T(8,128)}) custom-call(s32[1]{0:T(128)S(6)} %copy.26.args_0_, bf16[576,512]{1,0:T(8,128)(2,1)} %bitcast.18, bf16[576,512]{1,0:T(8,128)(2,1)} %bitcast.19, f32[576]{0:T(1024)} %args_3_.4, f32[576]{0:T(1024)} %args_4_.4, ...), custom_call_target="tpu_custom_call" | custom-call | tf_op jit(solution)/shard_map/pallas_call | solution.py:885
  130.2 3.3 %shard_map.230 = (bf16[576,512]{1,0:T(8,128)(2,1)}, f32[576,512]{1,0:T(8,128)}, f32[576]{0:T(1024)}, f32[144,72]{1,0:T(8,128)}, f32[24,144]{1,0:T(8,128)}, /*ind...) custom-call(bf16[576,512]{1,0:T(8,128)(2,1)} %get-tuple-element.29.r, ...), custom_call_target="tpu_custom_call" | custom-call | tf_op jit(solution)/shard_map/pallas_call | solution.py:900

commit v2 on v1

--- a/solution.py
+++ b/solution.py
@@ -577,6 +577,13 @@
     return jnp.concatenate([line[QB * z : QB * z + QB], jnp.zeros((8, line.shape[1]), F32)], axis=0)
 
 
+def when(condition, action):
+    if condition is None:
+        action()
+    else:
+        pl.when(condition)(action)
+
+
 class Links:
     def __init__(self, refs):
         self.__dict__.update(refs)
@@ -596,6 +603,11 @@
         self.yn = (self.dp, 2 * self.z + 1 - self.y)
         self.peer = [None] + [lax.rem(self.z + k, 4) for k in (1, 2, 3)]
         self.zn = [None] + [(self.dp, 2 * self.peer[k] + self.y) for k in (1, 2, 3)]
+        self.side = [None, (self.dp, 2 * (self.z + 1) + self.y), (self.dp, 2 * (self.z - 1) + self.y)]
+        self.here = {(sign, t): (self.z + sign * t >= 0) & (self.z + sign * t < 4) for sign in (1, -1) for t in (1, 2, 3)}
+        self.on = {(-1, 0): self.z < 3, (1, 0): self.z > 0}
+        for sign, t in self.here:
+            self.on[sign, t] = self.here[sign, t] & self.on[sign, 0]
         self.copies = {}
         self.used = 0
 
@@ -606,7 +618,7 @@
     def met(self):
         pl.semaphore_wait(pltpu.get_barrier_semaphore(), 6)
 
-    def send(self, name, src, dst, device):
+    def send(self, name, src, dst, device, condition=None):
         index = self.used
         self.used += 1
 
@@ -620,16 +632,16 @@
                 device_id_type=MESH,
             )
 
-        copy().start()
-        self.copies[name] = copy
-
-    def arrived(self, *names):
+        when(condition, lambda: copy().start())
+        self.copies[name] = (copy, condition)
+
+    def arrived(self, *names, condition=None):
         for name in names:
-            self.copies[name]().wait_recv()
+            when(condition, lambda name=name: self.copies[name][0]().wait_recv())
 
     def finish(self):
-        for copy in self.copies.values():
-            copy().wait_send()
+        for copy, condition in self.copies.values():
+            when(condition, lambda copy=copy: copy().wait_send())
 
     def run_if(self, condition, steps):
         if steps:
@@ -645,16 +657,39 @@
         block = lambda: region(self.weights, p, self.dp if dp is None else dp, self.y if y is None else y, z, count)
         self.send(("w", p, tag), block, block, device)
 
+    def block(self, p, z):
+        if p[0] in "OD":
+            return getattr(self, "slip" + p).at[z]
+        return region(self.weights, p, self.dp, self.y, z, 1)
+
+    def hop(self, p, t):
+        for tag, sign in (("r", -1), ("l", 1)):
+            here = self.here.get((sign, t))
+            if t > 0:
+                self.arrived(("w", p, tag, t - 1), condition=here)
+            block = lambda sign=sign: self.block(p, self.z + sign * t)
+            if t < 3:
+                self.send(("w", p, tag, t), block, block, self.side[-sign], self.on[sign, t])
+            if p[0] in "AG" and t > 0:
+                self.send(("w", p, "x", tag, t), block, block, self.xn, here)
+                self.send(("w", p, "y", tag, t), block, block, self.yn, here)
+
+    def own(self, p):
+        for axis, device in (("x", self.xn), ("y", self.yn)):
+            block = lambda: self.block(p, self.z)
+            self.send(("w", p, axis, "r", 0), block, block, device)
+
     def share(self, p):
-        for k in (1, 3, 2):
-            if p[0] in "OD":
-                block = lambda: getattr(self, "slip" + p).at[self.z]
-                self.send(("w", p, f"z{k}"), block, block, self.zn[k])
-            else:
-                self.spread(f"z{k}", p, self.zn[k], z=self.z, count=1)
+        self.hop(p, 0)
+
+    def one(self, p):
+        self.hop(p, 1)
+
+    def two(self, p):
+        self.hop(p, 2)
 
     def line(self, p):
-        self.arrived(*[("w", p, f"z{k}") for k in (1, 2, 3)])
+        self.hop(p, 3)
         if p[0] in "OD":
             slips = [getattr(self, "slip" + p)[z].astype(F32) for z in range(4)]
             if p == "O":
@@ -662,15 +697,24 @@
             else:
                 whole = jnp.concatenate([slip[:QB] for slip in slips], axis=0)
             region(self.weights, p, self.dp, self.y)[...] = whole.astype(BF)
-        self.spread("x", p, self.xn)
-        self.spread("y", p, self.yn)
+            self.spread("x", p, self.xn)
+            self.spread("y", p, self.yn)
         self.spread("s", p, self.sib)
 
+    def across(self, p, axis):
+        if p[0] in "OD":
+            self.arrived(("w", p, axis))
+            return
+        for t in range(4):
+            for tag, sign in (("r", -1), ("l", 1)):
+                if t > 0 or sign < 0:
+                    self.arrived(("w", p, axis, tag, t), condition=self.here.get((sign, t)))
+
     def cross(self, p):
-        self.arrived(("w", p, "x"))
+        self.across(p, "x")
         self.spread("xy", p, self.yn, dp=self.far, count=2)
         self.spread("sx", p, self.sib, dp=self.far)
-        self.arrived(("w", p, "y"))
+        self.across(p, "y")
         self.spread("yx", p, self.xn, y=self.ny, z=2, count=2)
         self.spread("sy", p, self.sib, y=self.ny)
 
@@ -789,7 +833,7 @@
     return shapes
 
 
-COPIES = len(PIECES) * (12 + 13) + 6
+COPIES = len(PIECES) * (6 + 14 + 7 + 13) + 6
 
 
 def pack_own(links, refs):
@@ -808,16 +852,13 @@
             region(links.weights, p, links.dp, links.y, links.z, 1)[...] = whole[p].astype(BF)
 
 
-BEGIN = ("share A0", "share A1", "share O", "share G0", "share G1", "share G2", "share D0", "share D1")
-BEFORE_PROJECT = (
-    "line A0", "line A1", "cross A0", "line O", "cross A1", "line G0", "rest A0", "cross O", "line G1", "rest A1", "line G2",
-    "end A0", "end A1",
-)
-AFTER_PROJECT = ("cross G0", "rest O")
-HEADS = (("line D0", "cross G1"), ("rest G0", "line D1"), ("end O", "cross G2"))
+BEGIN = ("own A1", "share A1", "own A0", "share A0", "own G1", "own G2", "own G0", "share G0")
+BEFORE_PROJECT = ("share G2", "one A1", "one A0", "share G1", "one G0", "one G2", "two A1", "two A0", "share O", "two G0", "two G2", "line A1", "line A0", "one G1", "share D1", "line G0", "one O", "line G2", "cross A1", "share D0", "two G1", "one D1", "cross A0", "two O", "cross G0", "line G1", "two D1", "one D0", "rest A0", "cross G2", "line O", "end A0", "rest A1", "two D0", "cross G1", "end A1")
+AFTER_PROJECT = ("line D1", "cross O", "line D0")
+HEADS = ((), ("rest G0", "rest G1", "rest G2", "rest O"), ("cross D1", "end O", "end G0"))
 BEFORE_OUT = ()
-BEFORE_MLP = ("rest G1", "cross D0", "rest G2", "end G0", "end G1", "end G2")
-MLP = (("cross D1", "rest D0"), ("rest D1", "end D0", "end D1"))
+BEFORE_MLP = ("end G1", "end G2", "cross D0")
+MLP = (("rest D1",), ("rest D0", "end D0", "end D1"))
 AFTER_DOWN = ("sibs D1", "sibs D0")
 HIDDEN = (("pair D1",), ("pair D0",), (), ())
 AFTER_GATE = (("sibs G0", "twos D1"), ("sibs G1",), ("pair G0", "sibs G2", "twos D0"))

time: 134 us -> 128 us (0.955)
  Pallas kernels: 132 us -> 127 us
    pallas_call x1, Pallas kernels: 129 us -> 124 us  [whole(): pl.pallas_call(functools.partial(whole_kernel, order, names), out_shape=[...]
where the time goes in v2:
time: 128 us
  Pallas kernels  127 us (99%)
  between operations  1.42 us (1%)
    pallas_call x1, Pallas kernels, whole(): pl.pallas_call(functools.partial(whole_kernel, order, names), out_shape=[...  124 us
    pallas_call x1, Pallas kernels, whole(): pl.pallas_call(finish_kernel, out_shape=[jax.ShapeDtypeStruct(*s) for s i...  3.31 us

profile of v2, /device:TPU:0, one launch (start us, length us, event | category | flops | bytes accessed | tf_op | source)
XLA Modules:
  0.0 128.3 jit_solution(864551900201541231)
XLA Ops:
  1.3 123.6 %shard_map.229 = (bf16[576,512]{1,0:T(8,128)(2,1)}, f32[576,512]{1,0:T(8,128)}, f32[144,640]{1,0:T(8,128)}, f32[72,384]{1,0:T(8,128)}, f32[8,576]{1,0:T(8,128)}) custom-call(s32[1]{0:T(128)S(6)} %copy.26.args_0_, bf16[576,512]{1,0:T(8,128)(2,1)} %bitcast.18, bf16[576,512]{1,0:T(8,128)(2,1)} %bitcast.19, f32[576]{0:T(1024)} %args_3_.4, f32[576]{0:T(1024)} %args_4_.4, ...), custom_call_target="tpu_custom_call" | custom-call | tf_op jit(solution)/shard_map/pallas_call | solution.py:926
  124.9 3.3 %shard_map.230 = (bf16[576,512]{1,0:T(8,128)(2,1)}, f32[576,512]{1,0:T(8,128)}, f32[576]{0:T(1024)}, f32[144,72]{1,0:T(8,128)}, f32[24,144]{1,0:T(8,128)}, /*ind...) custom-call(bf16[576,512]{1,0:T(8,128)(2,1)} %get-tuple-element.29.r, ...), custom_call_target="tpu_custom_call" | custom-call | tf_op jit(solution)/shard_map/pallas_call | solution.py:941

commit v3 on v2

--- a/solution.py
+++ b/solution.py
@@ -92,14 +92,19 @@
         lax.fori_loop(0, D // 64, clear, 0)
 
     def norm(self, src, r, gain, dst, rho_ref, row):
-        for ts in lane_tiles():
-            v = src[r, :, ts]
-            total = jnp.sum(v * v, axis=0, keepdims=True)
-            if row is not None:
-                self.stat[r, row : row + 1, ts] = total
-            rho = lax.rsqrt(total * (1.0 / D) + EPS)
-            rho_ref[r, 0:1, ts] = rho
-            dst[r, :, ts] = (v * rho * gain[...]).astype(BF)
+        total = jnp.zeros((8, T), F32)
+        for i in range(0, D, 8):
+            v = src[r, i : i + 8, :]
+            total = total + v * v
+        total = jnp.sum(total, axis=0, keepdims=True)
+        if row is not None:
+            self.stat[r, row : row + 1, :] = total
+        rho = lax.rsqrt(total * (1.0 / D) + EPS)
+        rho_ref[r, 0:1, :] = rho
+        for i in range(0, D, 64):
+            rows = slice(i, i + 64)
+            wide = jnp.concatenate([gain[rows, :]] * 4, axis=1)
+            dst[r, rows, :] = (src[r, rows, :] * rho * wide).astype(BF)
 
     def natural_rows(self, ref, base, width, first, count):
         pieces = []
@@ -288,12 +293,24 @@
         dst[index] = (value + dst[index].astype(F32)).astype(dst.dtype)
 
     def norm_back(self, src, r, rho_ref, gain, slot):
-        for ts in lane_tiles():
-            e, v, rho = self.E[:, ts], src[r, :, ts], rho_ref[r, 0:1, ts]
-            u = e * gain[...]
-            mean = jnp.sum(u * v, axis=0, keepdims=True) * (1.0 / D)
-            self.gacc[slot] += e * (v * rho)
-            self.G[:, ts] = self.G[:, ts] + rho * (u - v * (rho * rho * mean))
+        rho = rho_ref[r, 0:1, :]
+        total = jnp.zeros((8, T), F32)
+        for i in range(0, D, 64):
+            rows = slice(i, i + 64)
+            wide = jnp.concatenate([gain[rows, :]] * 4, axis=1)
+            e, v = self.E[rows, :], src[r, rows, :]
+            product = e * v
+            weighted = product * wide
+            for k in range(0, 64, 8):
+                total = total + weighted[k : k + 8]
+            share = product * rho
+            self.gacc[slot, rows, :] += share[:, :128] + share[:, 128:256] + share[:, 256:384] + share[:, 384:]
+        mean = jnp.sum(total, axis=0, keepdims=True) * (1.0 / D)
+        back = rho * rho * mean
+        for i in range(0, D, 64):
+            rows = slice(i, i + 64)
+            wide = jnp.concatenate([gain[rows, :]] * 4, axis=1)
+            self.G[rows, :] += rho * (self.E[rows, :] * wide - src[r, rows, :] * back)
 
     def mlp_back(self, r, links):
         self.pack_down()
@@ -860,18 +877,15 @@
 BEFORE_MLP = ("end G1", "end G2", "cross D0")
 MLP = (("rest D1",), ("rest D0", "end D0", "end D1"))
 AFTER_DOWN = ("sibs D1", "sibs D0")
-HIDDEN = (("pair D1",), ("pair D0",), (), ())
-AFTER_GATE = (("sibs G0", "twos D1"), ("sibs G1",), ("pair G0", "sibs G2", "twos D0"))
-BEFORE_NORM = ("pair G1", "twos G0")
-AFTER_OUT = ("sibs O", "pair G2")
-BEFORE_HEADS = ("fours D1",)
-BACK_HEADS = (("twos G1", "pair O"), ("fours D0", "twos G2"), ("fours G0", "twos O"))
+HIDDEN = (("pair D1",), (), ("pair D0",), ())
+AFTER_GATE = (("sibs G0",), ("sibs G1", "twos D1"), ("sibs G2", "pair G0"))
+BEFORE_NORM = ("twos D0", "pair G1")
+AFTER_OUT = ("sibs O", "fours D1")
+BEFORE_HEADS = ("twos G0",)
+BACK_HEADS = (("pair G2", "pair O", "fours D0"), ("twos G1", "fours G0"), ("twos G2", "twos O"))
 AFTER_QKV = ("sibs A0", "sibs A1", "fours G1", "pair A0", "pair A1")
-LAST = (
-    "tiny 0", "fours G2", "fours O", "tiny 1", "total D1", "total D0", "twos A0", "tiny 2", "twos A1", "total G0",
-)
-VERY_LAST = ("fours A0", "total G1", "tiny 3", "total G2", "total O", "fours A1", "total A0", "total A1")
-
+LAST = ("tiny 0", "fours G2", "fours O", "tiny 1", "twos A0", "tiny 2", "twos A1", "total D1", "total D0", "total G0")
+VERY_LAST = ("fours A0", "tiny 3", "total G1", "fours A1", "total G2", "total O", "total A0", "total A1")
 
 def whole_kernel(order, names, *args):
     refs = dict(zip(names, args))

time: 128 us -> 126 us (0.984)
  Pallas kernels: 127 us -> 125 us
    pallas_call x1, Pallas kernels: 124 us -> 121 us  [whole(): pl.pallas_call(functools.partial(whole_kernel, order, names), out_shape=[...]
where the time goes in v3:
time: 126 us
  Pallas kernels  125 us (99%)
  between operations  1.42 us (1%)
    pallas_call x1, Pallas kernels, whole(): pl.pallas_call(functools.partial(whole_kernel, order, names), out_shape=[...  121 us
    pallas_call x1, Pallas kernels, whole(): pl.pallas_call(finish_kernel, out_shape=[jax.ShapeDtypeStruct(*s) for s i...  3.31 us

profile of v3, /device:TPU:0, one launch (start us, length us, event | category | flops | bytes accessed | tf_op | source)
XLA Modules:
  0.0 126.0 jit_solution(2889999034495468715)
XLA Ops:
  1.3 121.2 %shard_map.229 = (bf16[576,512]{1,0:T(8,128)(2,1)}, f32[576,512]{1,0:T(8,128)}, f32[144,640]{1,0:T(8,128)}, f32[72,384]{1,0:T(8,128)}, f32[8,576]{1,0:T(8,128)}) custom-call(s32[1]{0:T(128)S(6)} %copy.26.args_0_, bf16[576,512]{1,0:T(8,128)(2,1)} %bitcast.18, bf16[576,512]{1,0:T(8,128)(2,1)} %bitcast.19, f32[576]{0:T(1024)} %args_3_.4, f32[576]{0:T(1024)} %args_4_.4, ...), custom_call_target="tpu_custom_call" | custom-call | tf_op jit(solution)/shard_map/pallas_call | solution.py:940
  122.5 3.3 %shard_map.230 = (bf16[576,512]{1,0:T(8,128)(2,1)}, f32[576,512]{1,0:T(8,128)}, f32[576]{0:T(1024)}, f32[144,72]{1,0:T(8,128)}, f32[24,144]{1,0:T(8,128)}, /*ind...) custom-call(bf16[576,512]{1,0:T(8,128)(2,1)} %get-tuple-element.29.r, ...), custom_call_target="tpu_custom_call" | custom-call | tf_op jit(solution)/shard_map/pallas_call | solution.py:955

commit v4 on v3

--- a/solution.py
+++ b/solution.py
@@ -484,6 +484,9 @@
     def run_if(self, condition, steps):
         pass
 
+    def written(self):
+        pass
+
 
 def applications(w, links):
     def forward(r, carry):
@@ -507,6 +510,7 @@
 
     lax.fori_loop(0, 2, forward, 0)
     w.write_output()
+    links.written()
     lax.fori_loop(0, 2, backward, 0)
 
 
@@ -628,6 +632,12 @@
         self.copies = {}
         self.used = 0
 
+    def written(self):
+        pltpu.make_async_copy(self.out, self.outfar, self.home.at[0]).start()
+
+    def turned(self):
+        pltpu.make_async_copy(self.G, self.gin, self.home.at[1]).start()
+
     def greet(self):
         for device in [self.sib, self.xn, self.yn] + self.zn[1:]:
             pl.semaphore_signal(pltpu.get_barrier_semaphore(), inc=1, device_id=device, device_id_type=MESH)
@@ -657,6 +667,8 @@
             when(condition, lambda name=name: self.copies[name][0]().wait_recv())
 
     def finish(self):
+        pltpu.make_async_copy(self.out, self.outfar, self.home.at[0]).wait()
+        pltpu.make_async_copy(self.G, self.gin, self.home.at[1]).wait()
         for copy, condition in self.copies.values():
             when(condition, lambda copy=copy: copy().wait_send())
 
@@ -882,8 +894,8 @@
 BEFORE_NORM = ("twos D0", "pair G1")
 AFTER_OUT = ("sibs O", "fours D1")
 BEFORE_HEADS = ("twos G0",)
-BACK_HEADS = (("pair G2", "pair O", "fours D0"), ("twos G1", "fours G0"), ("twos G2", "twos O"))
-AFTER_QKV = ("sibs A0", "sibs A1", "fours G1", "pair A0", "pair A1")
+BACK_HEADS = (("pair G2", "twos G1", "pair O"), ("fours D0", "twos G2", "fours G0"), ("twos O", "fours G1"))
+AFTER_QKV = ("sibs A0", "sibs A1", "pair A0", "pair A1")
 LAST = ("tiny 0", "fours G2", "fours O", "tiny 1", "twos A0", "tiny 2", "twos A1", "total D1", "total D0", "total G0")
 VERY_LAST = ("fours A0", "tiny 3", "total G1", "fours A1", "total G2", "total O", "total A0", "total A1")
 
@@ -896,9 +908,9 @@
     links.run(*BEGIN)
     w.start()
     applications(w, links)
+    links.turned()
     links.tinies[0] = w.small()
     links.run(*LAST)
-    w.write_grad()
     links.run(*VERY_LAST)
     links.tiny_end()
     links.finish()
@@ -932,18 +944,18 @@
         q=q, k=k.T, v=v.T, o=o, g=g, u=u, d=d.T,
     )
     outs = dict(
-        out=((D, T), BF), gin=((D, T), F32), sumN=((ROWS, 256 + 2 * FB), F32), sumD=((QB, LANES), F32), sumT=((8, D), F32)
+        outfar=((D, T), BF), gin=((D, T), F32), sumN=((ROWS, 256 + 2 * FB), F32), sumD=((QB, LANES), F32), sumT=((8, D), F32)
     )
-    scratch = dict(SCRATCH, **WEIGHTS, **GRADS, **rooms())
-    names = list(ins) + list(outs) + list(scratch) + ["sent", "came"]
+    scratch = dict(SCRATCH, out=((D, T), BF), **WEIGHTS, **GRADS, **rooms())
+    names = list(ins) + list(outs) + list(scratch) + ["sent", "came", "home"]
     vmem = pl.BlockSpec(memory_space=pltpu.VMEM)
     r = pl.pallas_call(
         functools.partial(whole_kernel, order, names),
         out_shape=[jax.ShapeDtypeStruct(*s) for s in outs.values()],
         in_specs=[pl.BlockSpec(memory_space=pltpu.SMEM)] + [vmem] * (len(ins) - 1),
-        out_specs=[vmem] * len(outs),
+        out_specs=[pl.BlockSpec(memory_space=pl.ANY)] * 2 + [vmem] * (len(outs) - 2),
         scratch_shapes=[pltpu.VMEM(*s) for s in scratch.values()]
-        + [pltpu.SemaphoreType.DMA((COPIES,)), pltpu.SemaphoreType.DMA((COPIES,))],
+        + [pltpu.SemaphoreType.DMA((n,)) for n in (COPIES, COPIES, 2)],
         compiler_params=pltpu.CompilerParams(
             vmem_limit_bytes=VMEM_LIMIT, collective_id=0, has_side_effects=True
         ),

time: 126 us -> 126 us (level)
  no operation moved by 1% of the time
where the time goes in v4:
time: 126 us; the launch traced here: 125 us
  Pallas kernels  124 us (98%)
  between operations  1.42 us (1%)
    pallas_call x1, Pallas kernels, whole(): pl.pallas_call(functools.partial(whole_kernel, order, names), out_shape=[...  121 us
    pallas_call x1, Pallas kernels, whole(): pl.pallas_call(finish_kernel, out_shape=[jax.ShapeDtypeStruct(*s) for s i...  3.31 us

profile of v4, /device:TPU:0, one launch (start us, length us, event | category | flops | bytes accessed | tf_op | source)
XLA Modules:
  0.0 125.3 jit_solution(10995585545523797156)
XLA Ops:
  1.3 120.6 %shard_map.229 = (bf16[576,512]{1,0:T(8,128)(2,1)}, f32[576,512]{1,0:T(8,128)}, f32[144,640]{1,0:T(8,128)}, f32[72,384]{1,0:T(8,128)}, f32[8,576]{1,0:T(8,128)}) custom-call(s32[1]{0:T(128)S(6)} %copy.26.args_0_, bf16[576,512]{1,0:T(8,128)(2,1)} %bitcast.18, bf16[576,512]{1,0:T(8,128)(2,1)} %bitcast.19, f32[576]{0:T(1024)} %args_3_.4, f32[576]{0:T(1024)} %args_4_.4, ...), custom_call_target="tpu_custom_call" | custom-call | tf_op jit(solution)/shard_map/pallas_call | solution.py:952
  121.9 3.3 %shard_map.230 = (bf16[576,512]{1,0:T(8,128)(2,1)}, f32[576,512]{1,0:T(8,128)}, f32[576]{0:T(1024)}, f32[144,72]{1,0:T(8,128)}, f32[24,144]{1,0:T(8,128)}, /*ind...) custom-call(bf16[576,512]{1,0:T(8,128)(2,1)} %get-tuple-element.29.r, ...), custom_call_target="tpu_custom_call" | custom-call | tf_op jit(solution)/shard_map/pallas_call | solution.py:967
